TPU v7x, 256 devices: a whole 4x4x8 slice. The times are simulated.
256 devices in a mesh: depth: 8 (over z_hi, core), tile: 32 (over y, x, z_lo).
Axes of the slice: x: 4, y: 4, z: 8 (z_hi: 4, z_lo: 2; z = z_hi * 2 + z_lo), core: 2. Of those that a mesh axis runs over, the one named last changes fastest.
Arguments:
- surface: float32 [4, 2, 2, 4, 1024, 128], P(None, None, None, None, 'tile'), may hold values from -5 to 5
- speeds: int32 [16, 1024, 128], P('depth', 'tile'), may hold values from 0 to 127
- table: float32 [16, 2, 8, 128], replicated, may hold values from -1 to 1
Outputs:
- image: float32 [16, 1024, 128], P('depth', 'tile')
All inputs are finite; a program needn't handle non-finite values.
Results may differ from a plain program's by a relative error of at most 0.0003.
Values sent between devices are 32-bit elements; how exact they have to be, the bound alone decides.
A program may use at most 64 MiB of HBM per device.

v0:
```python
import jax
import jax.numpy as jnp
from jax import lax
from jax.sharding import PartitionSpec as P


def padded_2(array, sides, width):
    for axis, dim in sides:
        devices, length = (lax.axis_size(axis), array.shape[dim])
        up = [(i, (i + 1) % devices) for i in range(devices - 1)]
        down = [(j, i) for i, j in up]
        last = lax.slice_in_dim(array, length - width, length, axis=dim)
        initial = lax.slice_in_dim(array, 0, width, axis=dim)
        before = lax.ppermute(last, axis, up)
        after = lax.ppermute(initial, axis, down)
        array = jnp.concatenate([before, array, after], axis=dim)
    return array


def from_behind(value, axis, steps):
    count = lax.axis_size(axis)
    initial, last = (max(0, -steps), min(count, count - steps))
    return lax.ppermute(value, axis, [(source, source + steps) for source in range(initial, last)])


def mcclellan(field):
    lead = [(0, 0)] * (field.ndim - 2)
    padded = jnp.pad(field, lead + [(1, 1), (0, 0)])
    along_rows = field + 0.5 * (padded[..., 2:, :] + padded[..., :-2, :])
    padded = jnp.pad(along_rows, lead + [(0, 0), (1, 1)])
    along_columns = along_rows + 0.5 * (padded[..., :, 2:] + padded[..., :, :-2])
    return 0.5 * along_columns - field


def accumulate(totals, term, factors, index):
    cosine = factors[:, 0, index]
    sine = factors[:, 1, index]
    src_re = totals[0] + cosine * term[0, 0] - sine * term[0, 1]
    src_im = totals[1] + cosine * term[0, 1] + sine * term[0, 0]
    rec_re = totals[2] + cosine * term[1, 0] + sine * term[1, 1]
    rec_im = totals[3] + cosine * term[1, 1] - sine * term[1, 0]
    return (src_re, src_im, rec_re, rec_im)


def chebyshev_sum(wide, factors, row_mask, offset, out_rows):
    terms = factors.shape[2]

    def inner(block):
        return lax.slice_in_dim(block, offset, offset + out_rows, axis=3)

    zero = jnp.zeros(factors[:, 0, 0].shape, jnp.float32)
    totals = accumulate((zero, zero, zero, zero), inner(wide), factors, 0)
    older = wide
    newer = mcclellan(wide) * row_mask
    totals = accumulate(totals, inner(newer), factors, 1)
    for index in range(2, terms):
        older, newer = (newer, (2.0 * mcclellan(newer) - older) * row_mask)
        totals = accumulate(totals, inner(newer), factors, index)
    return jnp.stack([jnp.stack([totals[0], totals[1]]), jnp.stack([totals[2], totals[3]])])


def selector_of(velocity, levels):
    height, width = velocity.shape
    flat_speed = velocity.reshape(1, height * width)
    return (lax.broadcasted_iota(jnp.int32, (levels, height * width), 0) == flat_speed).astype(
        jnp.float32
    )


def lookup(flat_table, selector, freqs, terms, height, width):
    picked = jnp.dot(
        flat_table, selector, preferred_element_type=jnp.float32, precision=lax.Precision.HIGHEST
    )
    return picked.reshape(freqs, 2, terms, height, width)


def rim_mask(height, margin, place, places):
    global_row = (
        place * height - margin + lax.broadcasted_iota(jnp.int32, (height + 2 * margin, 1), 0)
    )
    return ((global_row >= 0) & (global_row < places * height)).astype(jnp.float32)


def correlate(fields):
    return jnp.sum(fields[0, 0] * fields[1, 0] + fields[0, 1] * fields[1, 1], axis=0)


def body(surface, speeds, table):
    sections = lax.axis_size("depth")
    section = lax.axis_index("depth")
    places = lax.axis_size("tile")
    place = lax.axis_index("tile")
    batches = surface.shape[0]
    freqs = surface.shape[3]
    height = surface.shape[4]
    width = surface.shape[5]
    terms = table.shape[2]
    levels = table.shape[3]
    reach = terms - 1
    total_steps = batches + sections - 1
    near_mask = rim_mask(height, reach, place, places)
    selectors = [selector_of(speeds[level], levels) for level in range(speeds.shape[0])]

    def advance(step, state):
        incoming, image = state
        batch = step - section
        active = (batch >= 0) & (batch < batches)
        chosen = jnp.clip(batch, 0, batches - 1)
        fresh = lax.dynamic_index_in_dim(surface, chosen, 0, keepdims=False)
        fields = jnp.where(section == 0, fresh, incoming)
        flat_table = lax.dynamic_slice_in_dim(table, chosen * freqs, freqs, 0).reshape(-1, levels)
        layers = []
        for level in range(speeds.shape[0]):
            wide = padded_2(fields, (("tile", 3),), reach)
            factors = lookup(flat_table, selectors[level], freqs, terms, height, width)
            fields = chebyshev_sum(wide, factors, near_mask, reach, height)
            layers.append(correlate(fields))
        image = image + jnp.where(active, jnp.stack(layers), 0.0)
        incoming = from_behind(fields, "depth", 1)
        return (incoming, image)

    start = (
        jnp.zeros((2, 2, freqs, height, width), jnp.float32),
        jnp.zeros((speeds.shape[0], height, width), jnp.float32),
    )
    final = lax.fori_loop(0, total_steps, advance, start)
    return final[1]


def solution(mesh):
    return jax.shard_map(
        body,
        mesh=mesh,
        in_specs=(P(None, None, None, None, "tile", None), P("depth", "tile", None), P()),
        out_specs=P("depth", "tile", None),
        check_vma=False,
    )
```

profile of v0, /device:TPU:89, one launch (start us, length us, event | category | flops | bytes accessed | tf_op | source)
XLA Modules:
  0.0 577.4 jit_solution(634475461020939302)
XLA Ops:
  1.4 576.0 %while.18 = (s32[]{:T(128)}, f32[2,2,4,32,128]{4,3,2,1,0:T(8,128)S(1)}, f32[2,32,128]{2,1,0:T(8,128)}, s32[]{:T(128)}, f32[16,2,8,128]{3,2,1,0:T(8,128)}, /*inde...) while((s32[]{:T(128)}, ...), condition=%wide.region_3.4_spmd.clone, body=%wide.region_0.3_spmd.clone.sunk | while | flops 827457792 | bytes 70077592 | solution.py:126
  27.4 6.4 %collective-permute-start.2 = (f32[2,2,4,7,128]{4,3,2,1,0:T(8,128)S(1)}, f32[2,2,4,7,128]{4,3,2,1,0:T(8,128)S(1)}, u32[]{:S(2)}, u32[]{:S(2)}) collective-permute-start(f32[2,2,4,7,128]{4,3,2,1,0:T(8,128)S(1)} %get-tuple-element.469), channel_id=1, source_target_pairs={{1,0},{2,1},{3,2},{4,3},{5,4},{6,5},{7,6},{8,7},{9,8},{10,9},{11,1... | collective-permute-start | bytes 172040 | tf_op jit(solution)/shard_map/while/body/eval_jaxpr/ppermute | solution.py:15
  35.7 6.1 %collective-permute-done.3 = f32[2,2,4,7,128]{4,3,2,1,0:T(8,128)S(1)} collective-permute-done((f32[2,2,4,7,128]{4,3,2,1,0:T(8,128)S(1)}, f32[2,2,4,7,128]{4,3,2,1,0:T(8,128)S(1)}, u32[]{:S(2)}, u32[]{:S(2)}) %collective-permute-start.3) | collective-permute-done | bytes 57376 | tf_op jit(solution)/shard_map/while/body/eval_jaxpr/ppermute | solution.py:14
  45.4 7.8 %collective-permute-start.4 = (f32[2,2,4,32,128]{4,3,2,1,0:T(8,128)S(1)}, f32[2,2,4,32,128]{4,3,2,1,0:T(8,128)S(1)}, u32[]{:S(2)}, u32[]{:S(2)}) collective-permute-start(f32[2,2,4,32,128]{4,3,2,1,0:T(8,128)S(1)} %pad_maximum_fusion.12), channel_id=1, source_target_pairs={{0,32},{32,64},{64,96},{96,128},{128,160},{160,192},{192,224},{1,3... | collective-permute-start | bytes 786440 | tf_op jit(solution)/shard_map/while/body/eval_jaxpr/ppermute | solution.py:23
  87.4 6.1 %collective-permute-done.3 = f32[2,2,4,7,128]{4,3,2,1,0:T(8,128)S(1)} collective-permute-done((f32[2,2,4,7,128]{4,3,2,1,0:T(8,128)S(1)}, f32[2,2,4,7,128]{4,3,2,1,0:T(8,128)S(1)}, u32[]{:S(2)}, u32[]{:S(2)}) %collective-permute-start.3) | collective-permute-done | bytes 57376 | tf_op jit(solution)/shard_map/while/body/eval_jaxpr/ppermute | solution.py:14
  97.1 8.5 %collective-permute-start.4 = (f32[2,2,4,32,128]{4,3,2,1,0:T(8,128)S(1)}, f32[2,2,4,32,128]{4,3,2,1,0:T(8,128)S(1)}, u32[]{:S(2)}, u32[]{:S(2)}) collective-permute-start(f32[2,2,4,32,128]{4,3,2,1,0:T(8,128)S(1)} %pad_maximum_fusion.12), channel_id=1, source_target_pairs={{0,32},{32,64},{64,96},{96,128},{128,160},{160,192},{192,224},{1,3... | collective-permute-start | bytes 786440 | tf_op jit(solution)/shard_map/while/body/eval_jaxpr/ppermute | solution.py:23
  132.3 6.1 %collective-permute-start.2 = (f32[2,2,4,7,128]{4,3,2,1,0:T(8,128)S(1)}, f32[2,2,4,7,128]{4,3,2,1,0:T(8,128)S(1)}, u32[]{:S(2)}, u32[]{:S(2)}) collective-permute-start(f32[2,2,4,7,128]{4,3,2,1,0:T(8,128)S(1)} %get-tuple-element.469), channel_id=1, source_target_pairs={{1,0},{2,1},{3,2},{4,3},{5,4},{6,5},{7,6},{8,7},{9,8},{10,9},{11,1... | collective-permute-start | bytes 172040 | tf_op jit(solution)/shard_map/while/body/eval_jaxpr/ppermute | solution.py:15
  140.3 6.2 %collective-permute-done.3 = f32[2,2,4,7,128]{4,3,2,1,0:T(8,128)S(1)} collective-permute-done((f32[2,2,4,7,128]{4,3,2,1,0:T(8,128)S(1)}, f32[2,2,4,7,128]{4,3,2,1,0:T(8,128)S(1)}, u32[]{:S(2)}, u32[]{:S(2)}) %collective-permute-start.3) | collective-permute-done | bytes 57376 | tf_op jit(solution)/shard_map/while/body/eval_jaxpr/ppermute | solution.py:14
  150.2 8.4 %collective-permute-start.4 = (f32[2,2,4,32,128]{4,3,2,1,0:T(8,128)S(1)}, f32[2,2,4,32,128]{4,3,2,1,0:T(8,128)S(1)}, u32[]{:S(2)}, u32[]{:S(2)}) collective-permute-start(f32[2,2,4,32,128]{4,3,2,1,0:T(8,128)S(1)} %pad_maximum_fusion.12), channel_id=1, source_target_pairs={{0,32},{32,64},{64,96},{96,128},{128,160},{160,192},{192,224},{1,3... | collective-permute-start | bytes 786440 | tf_op jit(solution)/shard_map/while/body/eval_jaxpr/ppermute | solution.py:23
  202.4 8.5 %collective-permute-start.4 = (f32[2,2,4,32,128]{4,3,2,1,0:T(8,128)S(1)}, f32[2,2,4,32,128]{4,3,2,1,0:T(8,128)S(1)}, u32[]{:S(2)}, u32[]{:S(2)}) collective-permute-start(f32[2,2,4,32,128]{4,3,2,1,0:T(8,128)S(1)} %pad_maximum_fusion.12), channel_id=1, source_target_pairs={{0,32},{32,64},{64,96},{96,128},{128,160},{160,192},{192,224},{1,3... | collective-permute-start | bytes 786440 | tf_op jit(solution)/shard_map/while/body/eval_jaxpr/ppermute | solution.py:23
  244.5 6.1 %collective-permute-done.3 = f32[2,2,4,7,128]{4,3,2,1,0:T(8,128)S(1)} collective-permute-done((f32[2,2,4,7,128]{4,3,2,1,0:T(8,128)S(1)}, f32[2,2,4,7,128]{4,3,2,1,0:T(8,128)S(1)}, u32[]{:S(2)}, u32[]{:S(2)}) %collective-permute-start.3) | collective-permute-done | bytes 57376 | tf_op jit(solution)/shard_map/while/body/eval_jaxpr/ppermute | solution.py:14
  254.2 8.2 %collective-permute-start.4 = (f32[2,2,4,32,128]{4,3,2,1,0:T(8,128)S(1)}, f32[2,2,4,32,128]{4,3,2,1,0:T(8,128)S(1)}, u32[]{:S(2)}, u32[]{:S(2)}) collective-permute-start(f32[2,2,4,32,128]{4,3,2,1,0:T(8,128)S(1)} %pad_maximum_fusion.12), channel_id=1, source_target_pairs={{0,32},{32,64},{64,96},{96,128},{128,160},{160,192},{192,224},{1,3... | collective-permute-start | bytes 786440 | tf_op jit(solution)/shard_map/while/body/eval_jaxpr/ppermute | solution.py:23
  296.1 6.1 %collective-permute-done.3 = f32[2,2,4,7,128]{4,3,2,1,0:T(8,128)S(1)} collective-permute-done((f32[2,2,4,7,128]{4,3,2,1,0:T(8,128)S(1)}, f32[2,2,4,7,128]{4,3,2,1,0:T(8,128)S(1)}, u32[]{:S(2)}, u32[]{:S(2)}) %collective-permute-start.3) | collective-permute-done | bytes 57376 | tf_op jit(solution)/shard_map/while/body/eval_jaxpr/ppermute | solution.py:14
  305.8 8.2 %collective-permute-start.4 = (f32[2,2,4,32,128]{4,3,2,1,0:T(8,128)S(1)}, f32[2,2,4,32,128]{4,3,2,1,0:T(8,128)S(1)}, u32[]{:S(2)}, u32[]{:S(2)}) collective-permute-start(f32[2,2,4,32,128]{4,3,2,1,0:T(8,128)S(1)} %pad_maximum_fusion.12), channel_id=1, source_target_pairs={{0,32},{32,64},{64,96},{96,128},{128,160},{160,192},{192,224},{1,3... | collective-permute-start | bytes 786440 | tf_op jit(solution)/shard_map/while/body/eval_jaxpr/ppermute | solution.py:23
  347.6 6.1 %collective-permute-done.3 = f32[2,2,4,7,128]{4,3,2,1,0:T(8,128)S(1)} collective-permute-done((f32[2,2,4,7,128]{4,3,2,1,0:T(8,128)S(1)}, f32[2,2,4,7,128]{4,3,2,1,0:T(8,128)S(1)}, u32[]{:S(2)}, u32[]{:S(2)}) %collective-permute-start.3) | collective-permute-done | bytes 57376 | tf_op jit(solution)/shard_map/while/body/eval_jaxpr/ppermute | solution.py:14
  357.3 8.3 %collective-permute-start.4 = (f32[2,2,4,32,128]{4,3,2,1,0:T(8,128)S(1)}, f32[2,2,4,32,128]{4,3,2,1,0:T(8,128)S(1)}, u32[]{:S(2)}, u32[]{:S(2)}) collective-permute-start(f32[2,2,4,32,128]{4,3,2,1,0:T(8,128)S(1)} %pad_maximum_fusion.12), channel_id=1, source_target_pairs={{0,32},{32,64},{64,96},{96,128},{128,160},{160,192},{192,224},{1,3... | collective-permute-start | bytes 786440 | tf_op jit(solution)/shard_map/while/body/eval_jaxpr/ppermute | solution.py:23
  399.8 6.1 %collective-permute-done.3 = f32[2,2,4,7,128]{4,3,2,1,0:T(8,128)S(1)} collective-permute-done((f32[2,2,4,7,128]{4,3,2,1,0:T(8,128)S(1)}, f32[2,2,4,7,128]{4,3,2,1,0:T(8,128)S(1)}, u32[]{:S(2)}, u32[]{:S(2)}) %collective-permute-start.3) | collective-permute-done | bytes 57376 | tf_op jit(solution)/shard_map/while/body/eval_jaxpr/ppermute | solution.py:14
  409.5 8.2 %collective-permute-start.4 = (f32[2,2,4,32,128]{4,3,2,1,0:T(8,128)S(1)}, f32[2,2,4,32,128]{4,3,2,1,0:T(8,128)S(1)}, u32[]{:S(2)}, u32[]{:S(2)}) collective-permute-start(f32[2,2,4,32,128]{4,3,2,1,0:T(8,128)S(1)} %pad_maximum_fusion.12), channel_id=1, source_target_pairs={{0,32},{32,64},{64,96},{96,128},{128,160},{160,192},{192,224},{1,3... | collective-permute-start | bytes 786440 | tf_op jit(solution)/shard_map/while/body/eval_jaxpr/ppermute | solution.py:23
  452.1 6.1 %collective-permute-done.3 = f32[2,2,4,7,128]{4,3,2,1,0:T(8,128)S(1)} collective-permute-done((f32[2,2,4,7,128]{4,3,2,1,0:T(8,128)S(1)}, f32[2,2,4,7,128]{4,3,2,1,0:T(8,128)S(1)}, u32[]{:S(2)}, u32[]{:S(2)}) %collective-permute-start.3) | collective-permute-done | bytes 57376 | tf_op jit(solution)/shard_map/while/body/eval_jaxpr/ppermute | solution.py:14
  461.8 8.2 %collective-permute-start.4 = (f32[2,2,4,32,128]{4,3,2,1,0:T(8,128)S(1)}, f32[2,2,4,32,128]{4,3,2,1,0:T(8,128)S(1)}, u32[]{:S(2)}, u32[]{:S(2)}) collective-permute-start(f32[2,2,4,32,128]{4,3,2,1,0:T(8,128)S(1)} %pad_maximum_fusion.12), channel_id=1, source_target_pairs={{0,32},{32,64},{64,96},{96,128},{128,160},{160,192},{192,224},{1,3... | collective-permute-start | bytes 786440 | tf_op jit(solution)/shard_map/while/body/eval_jaxpr/ppermute | solution.py:23
  504.3 6.1 %collective-permute-done.3 = f32[2,2,4,7,128]{4,3,2,1,0:T(8,128)S(1)} collective-permute-done((f32[2,2,4,7,128]{4,3,2,1,0:T(8,128)S(1)}, f32[2,2,4,7,128]{4,3,2,1,0:T(8,128)S(1)}, u32[]{:S(2)}, u32[]{:S(2)}) %collective-permute-start.3) | collective-permute-done | bytes 57376 | tf_op jit(solution)/shard_map/while/body/eval_jaxpr/ppermute | solution.py:14
  514.0 8.2 %collective-permute-start.4 = (f32[2,2,4,32,128]{4,3,2,1,0:T(8,128)S(1)}, f32[2,2,4,32,128]{4,3,2,1,0:T(8,128)S(1)}, u32[]{:S(2)}, u32[]{:S(2)}) collective-permute-start(f32[2,2,4,32,128]{4,3,2,1,0:T(8,128)S(1)} %pad_maximum_fusion.12), channel_id=1, source_target_pairs={{0,32},{32,64},{64,96},{96,128},{128,160},{160,192},{192,224},{1,3... | collective-permute-start | bytes 786440 | tf_op jit(solution)/shard_map/while/body/eval_jaxpr/ppermute | solution.py:23
  556.2 6.1 %collective-permute-done.3 = f32[2,2,4,7,128]{4,3,2,1,0:T(8,128)S(1)} collective-permute-done((f32[2,2,4,7,128]{4,3,2,1,0:T(8,128)S(1)}, f32[2,2,4,7,128]{4,3,2,1,0:T(8,128)S(1)}, u32[]{:S(2)}, u32[]{:S(2)}) %collective-permute-start.3) | collective-permute-done | bytes 57376 | tf_op jit(solution)/shard_map/while/body/eval_jaxpr/ppermute | solution.py:14
  565.9 8.2 %collective-permute-start.4 = (f32[2,2,4,32,128]{4,3,2,1,0:T(8,128)S(1)}, f32[2,2,4,32,128]{4,3,2,1,0:T(8,128)S(1)}, u32[]{:S(2)}, u32[]{:S(2)}) collective-permute-start(f32[2,2,4,32,128]{4,3,2,1,0:T(8,128)S(1)} %pad_maximum_fusion.12), channel_id=1, source_target_pairs={{0,32},{32,64},{64,96},{96,128},{128,160},{160,192},{192,224},{1,3... | collective-permute-start | bytes 786440 | tf_op jit(solution)/shard_map/while/body/eval_jaxpr/ppermute | solution.py:23
  (695 shorter events, 409.0 us)
Async XLA Ops:
  3.0 20.7 %collective-permute-start = (f32[2,2,4,7,128]{4,3,2,1,0:T(8,128)}, f32[2,2,4,7,128]{4,3,2,1,0:T(8,128)S(1)}, u32[]{:S(2)}, u32[]{:S(2)}) collective-permute-start(f32[2,2,4,7,128]{4,3,2,1,0:T(8,128)} %get-tuple-element.467), channel_id=1, source_target_pairs={{1,0},{2,1},{3,2},{4,3},{5,4},{6,5},{7,6},{8,7},{9,8},{10,9},{11,1... | collective-permute-start | bytes 172040 | tf_op jit(solution)/shard_map/while/body/eval_jaxpr/ppermute | solution.py:15
  9.0 14.8 %collective-permute-start.1 = (f32[2,2,4,7,128]{4,3,2,1,0:T(8,128)}, f32[2,2,4,7,128]{4,3,2,1,0:T(8,128)S(1)}, u32[]{:S(2)}, u32[]{:S(2)}) collective-permute-start(f32[2,2,4,7,128]{4,3,2,1,0:T(8,128)} %get-tuple-element.468), channel_id=1, source_target_pairs={{0,1},{1,2},{2,3},{3,4},{4,5},{5,6},{6,7},{7,8},{8,9},{9,10},{10,1... | collective-permute-start | bytes 172040 | tf_op jit(solution)/shard_map/while/body/eval_jaxpr/ppermute | solution.py:14
  58.1 18.1 %collective-permute-start = (f32[2,2,4,7,128]{4,3,2,1,0:T(8,128)}, f32[2,2,4,7,128]{4,3,2,1,0:T(8,128)S(1)}, u32[]{:S(2)}, u32[]{:S(2)}) collective-permute-start(f32[2,2,4,7,128]{4,3,2,1,0:T(8,128)} %get-tuple-element.467), channel_id=1, source_target_pairs={{1,0},{2,1},{3,2},{4,3},{5,4},{6,5},{7,6},{8,7},{9,8},{10,9},{11,1... | collective-permute-start | bytes 172040 | tf_op jit(solution)/shard_map/while/body/eval_jaxpr/ppermute | solution.py:15
  60.6 15.6 %collective-permute-start.1 = (f32[2,2,4,7,128]{4,3,2,1,0:T(8,128)}, f32[2,2,4,7,128]{4,3,2,1,0:T(8,128)S(1)}, u32[]{:S(2)}, u32[]{:S(2)}) collective-permute-start(f32[2,2,4,7,128]{4,3,2,1,0:T(8,128)} %get-tuple-element.468), channel_id=1, source_target_pairs={{0,1},{1,2},{2,3},{3,4},{4,5},{5,6},{6,7},{7,8},{8,9},{9,10},{10,1... | collective-permute-start | bytes 172040 | tf_op jit(solution)/shard_map/while/body/eval_jaxpr/ppermute | solution.py:14
  110.5 18.1 %collective-permute-start = (f32[2,2,4,7,128]{4,3,2,1,0:T(8,128)}, f32[2,2,4,7,128]{4,3,2,1,0:T(8,128)S(1)}, u32[]{:S(2)}, u32[]{:S(2)}) collective-permute-start(f32[2,2,4,7,128]{4,3,2,1,0:T(8,128)} %get-tuple-element.467), channel_id=1, source_target_pairs={{1,0},{2,1},{3,2},{4,3},{5,4},{6,5},{7,6},{8,7},{9,8},{10,9},{11,1... | collective-permute-start | bytes 172040 | tf_op jit(solution)/shard_map/while/body/eval_jaxpr/ppermute | solution.py:15
  113.6 15.1 %collective-permute-start.1 = (f32[2,2,4,7,128]{4,3,2,1,0:T(8,128)}, f32[2,2,4,7,128]{4,3,2,1,0:T(8,128)S(1)}, u32[]{:S(2)}, u32[]{:S(2)}) collective-permute-start(f32[2,2,4,7,128]{4,3,2,1,0:T(8,128)} %get-tuple-element.468), channel_id=1, source_target_pairs={{0,1},{1,2},{2,3},{3,4},{4,5},{5,6},{6,7},{7,8},{8,9},{9,10},{10,1... | collective-permute-start | bytes 172040 | tf_op jit(solution)/shard_map/while/body/eval_jaxpr/ppermute | solution.py:14
  163.5 18.1 %collective-permute-start = (f32[2,2,4,7,128]{4,3,2,1,0:T(8,128)}, f32[2,2,4,7,128]{4,3,2,1,0:T(8,128)S(1)}, u32[]{:S(2)}, u32[]{:S(2)}) collective-permute-start(f32[2,2,4,7,128]{4,3,2,1,0:T(8,128)} %get-tuple-element.467), channel_id=1, source_target_pairs={{1,0},{2,1},{3,2},{4,3},{5,4},{6,5},{7,6},{8,7},{9,8},{10,9},{11,1... | collective-permute-start | bytes 172040 | tf_op jit(solution)/shard_map/while/body/eval_jaxpr/ppermute | solution.py:15
  165.9 15.7 %collective-permute-start.1 = (f32[2,2,4,7,128]{4,3,2,1,0:T(8,128)}, f32[2,2,4,7,128]{4,3,2,1,0:T(8,128)S(1)}, u32[]{:S(2)}, u32[]{:S(2)}) collective-permute-start(f32[2,2,4,7,128]{4,3,2,1,0:T(8,128)} %get-tuple-element.468), channel_id=1, source_target_pairs={{0,1},{1,2},{2,3},{3,4},{4,5},{5,6},{6,7},{7,8},{8,9},{9,10},{10,1... | collective-permute-start | bytes 172040 | tf_op jit(solution)/shard_map/while/body/eval_jaxpr/ppermute | solution.py:14
  215.8 18.1 %collective-permute-start = (f32[2,2,4,7,128]{4,3,2,1,0:T(8,128)}, f32[2,2,4,7,128]{4,3,2,1,0:T(8,128)S(1)}, u32[]{:S(2)}, u32[]{:S(2)}) collective-permute-start(f32[2,2,4,7,128]{4,3,2,1,0:T(8,128)} %get-tuple-element.467), channel_id=1, source_target_pairs={{1,0},{2,1},{3,2},{4,3},{5,4},{6,5},{7,6},{8,7},{9,8},{10,9},{11,1... | collective-permute-start | bytes 172040 | tf_op jit(solution)/shard_map/while/body/eval_jaxpr/ppermute | solution.py:15
  217.8 16.2 %collective-permute-start.1 = (f32[2,2,4,7,128]{4,3,2,1,0:T(8,128)}, f32[2,2,4,7,128]{4,3,2,1,0:T(8,128)S(1)}, u32[]{:S(2)}, u32[]{:S(2)}) collective-permute-start(f32[2,2,4,7,128]{4,3,2,1,0:T(8,128)} %get-tuple-element.468), channel_id=1, source_target_pairs={{0,1},{1,2},{2,3},{3,4},{4,5},{5,6},{6,7},{7,8},{8,9},{9,10},{10,1... | collective-permute-start | bytes 172040 | tf_op jit(solution)/shard_map/while/body/eval_jaxpr/ppermute | solution.py:14
  267.4 18.1 %collective-permute-start = (f32[2,2,4,7,128]{4,3,2,1,0:T(8,128)}, f32[2,2,4,7,128]{4,3,2,1,0:T(8,128)S(1)}, u32[]{:S(2)}, u32[]{:S(2)}) collective-permute-start(f32[2,2,4,7,128]{4,3,2,1,0:T(8,128)} %get-tuple-element.467), channel_id=1, source_target_pairs={{1,0},{2,1},{3,2},{4,3},{5,4},{6,5},{7,6},{8,7},{9,8},{10,9},{11,1... | collective-permute-start | bytes 172040 | tf_op jit(solution)/shard_map/while/body/eval_jaxpr/ppermute | solution.py:15
  269.3 16.2 %collective-permute-start.1 = (f32[2,2,4,7,128]{4,3,2,1,0:T(8,128)}, f32[2,2,4,7,128]{4,3,2,1,0:T(8,128)S(1)}, u32[]{:S(2)}, u32[]{:S(2)}) collective-permute-start(f32[2,2,4,7,128]{4,3,2,1,0:T(8,128)} %get-tuple-element.468), channel_id=1, source_target_pairs={{0,1},{1,2},{2,3},{3,4},{4,5},{5,6},{6,7},{7,8},{8,9},{9,10},{10,1... | collective-permute-start | bytes 172040 | tf_op jit(solution)/shard_map/while/body/eval_jaxpr/ppermute | solution.py:14
  318.9 18.1 %collective-permute-start = (f32[2,2,4,7,128]{4,3,2,1,0:T(8,128)}, f32[2,2,4,7,128]{4,3,2,1,0:T(8,128)S(1)}, u32[]{:S(2)}, u32[]{:S(2)}) collective-permute-start(f32[2,2,4,7,128]{4,3,2,1,0:T(8,128)} %get-tuple-element.467), channel_id=1, source_target_pairs={{1,0},{2,1},{3,2},{4,3},{5,4},{6,5},{7,6},{8,7},{9,8},{10,9},{11,1... | collective-permute-start | bytes 172040 | tf_op jit(solution)/shard_map/while/body/eval_jaxpr/ppermute | solution.py:15
  320.8 16.2 %collective-permute-start.1 = (f32[2,2,4,7,128]{4,3,2,1,0:T(8,128)}, f32[2,2,4,7,128]{4,3,2,1,0:T(8,128)S(1)}, u32[]{:S(2)}, u32[]{:S(2)}) collective-permute-start(f32[2,2,4,7,128]{4,3,2,1,0:T(8,128)} %get-tuple-element.468), channel_id=1, source_target_pairs={{0,1},{1,2},{2,3},{3,4},{4,5},{5,6},{6,7},{7,8},{8,9},{9,10},{10,1... | collective-permute-start | bytes 172040 | tf_op jit(solution)/shard_map/while/body/eval_jaxpr/ppermute | solution.py:14
  371.2 18.1 %collective-permute-start = (f32[2,2,4,7,128]{4,3,2,1,0:T(8,128)}, f32[2,2,4,7,128]{4,3,2,1,0:T(8,128)S(1)}, u32[]{:S(2)}, u32[]{:S(2)}) collective-permute-start(f32[2,2,4,7,128]{4,3,2,1,0:T(8,128)} %get-tuple-element.467), channel_id=1, source_target_pairs={{1,0},{2,1},{3,2},{4,3},{5,4},{6,5},{7,6},{8,7},{9,8},{10,9},{11,1... | collective-permute-start | bytes 172040 | tf_op jit(solution)/shard_map/while/body/eval_jaxpr/ppermute | solution.py:15
  373.1 16.2 %collective-permute-start.1 = (f32[2,2,4,7,128]{4,3,2,1,0:T(8,128)}, f32[2,2,4,7,128]{4,3,2,1,0:T(8,128)S(1)}, u32[]{:S(2)}, u32[]{:S(2)}) collective-permute-start(f32[2,2,4,7,128]{4,3,2,1,0:T(8,128)} %get-tuple-element.468), channel_id=1, source_target_pairs={{0,1},{1,2},{2,3},{3,4},{4,5},{5,6},{6,7},{7,8},{8,9},{9,10},{10,1... | collective-permute-start | bytes 172040 | tf_op jit(solution)/shard_map/while/body/eval_jaxpr/ppermute | solution.py:14
  409.5 12.2 %collective-permute-start.4 = (f32[2,2,4,32,128]{4,3,2,1,0:T(8,128)S(1)}, f32[2,2,4,32,128]{4,3,2,1,0:T(8,128)S(1)}, u32[]{:S(2)}, u32[]{:S(2)}) collective-permute-start(f32[2,2,4,32,128]{4,3,2,1,0:T(8,128)S(1)} %pad_maximum_fusion.12), channel_id=1, source_target_pairs={{0,32},{32,64},{64,96},{96,128},{128,160},{160,192},{192,224},{1,3... | collective-permute-start | bytes 786440 | tf_op jit(solution)/shard_map/while/body/eval_jaxpr/ppermute | solution.py:23
  423.4 18.1 %collective-permute-start = (f32[2,2,4,7,128]{4,3,2,1,0:T(8,128)}, f32[2,2,4,7,128]{4,3,2,1,0:T(8,128)S(1)}, u32[]{:S(2)}, u32[]{:S(2)}) collective-permute-start(f32[2,2,4,7,128]{4,3,2,1,0:T(8,128)} %get-tuple-element.467), channel_id=1, source_target_pairs={{1,0},{2,1},{3,2},{4,3},{5,4},{6,5},{7,6},{8,7},{9,8},{10,9},{11,1... | collective-permute-start | bytes 172040 | tf_op jit(solution)/shard_map/while/body/eval_jaxpr/ppermute | solution.py:15
  425.3 16.2 %collective-permute-start.1 = (f32[2,2,4,7,128]{4,3,2,1,0:T(8,128)}, f32[2,2,4,7,128]{4,3,2,1,0:T(8,128)S(1)}, u32[]{:S(2)}, u32[]{:S(2)}) collective-permute-start(f32[2,2,4,7,128]{4,3,2,1,0:T(8,128)} %get-tuple-element.468), channel_id=1, source_target_pairs={{0,1},{1,2},{2,3},{3,4},{4,5},{5,6},{6,7},{7,8},{8,9},{9,10},{10,1... | collective-permute-start | bytes 172040 | tf_op jit(solution)/shard_map/while/body/eval_jaxpr/ppermute | solution.py:14
  461.8 12.2 %collective-permute-start.4 = (f32[2,2,4,32,128]{4,3,2,1,0:T(8,128)S(1)}, f32[2,2,4,32,128]{4,3,2,1,0:T(8,128)S(1)}, u32[]{:S(2)}, u32[]{:S(2)}) collective-permute-start(f32[2,2,4,32,128]{4,3,2,1,0:T(8,128)S(1)} %pad_maximum_fusion.12), channel_id=1, source_target_pairs={{0,32},{32,64},{64,96},{96,128},{128,160},{160,192},{192,224},{1,3... | collective-permute-start | bytes 786440 | tf_op jit(solution)/shard_map/while/body/eval_jaxpr/ppermute | solution.py:23
  475.7 18.1 %collective-permute-start = (f32[2,2,4,7,128]{4,3,2,1,0:T(8,128)}, f32[2,2,4,7,128]{4,3,2,1,0:T(8,128)S(1)}, u32[]{:S(2)}, u32[]{:S(2)}) collective-permute-start(f32[2,2,4,7,128]{4,3,2,1,0:T(8,128)} %get-tuple-element.467), channel_id=1, source_target_pairs={{1,0},{2,1},{3,2},{4,3},{5,4},{6,5},{7,6},{8,7},{9,8},{10,9},{11,1... | collective-permute-start | bytes 172040 | tf_op jit(solution)/shard_map/while/body/eval_jaxpr/ppermute | solution.py:15
  477.6 16.2 %collective-permute-start.1 = (f32[2,2,4,7,128]{4,3,2,1,0:T(8,128)}, f32[2,2,4,7,128]{4,3,2,1,0:T(8,128)S(1)}, u32[]{:S(2)}, u32[]{:S(2)}) collective-permute-start(f32[2,2,4,7,128]{4,3,2,1,0:T(8,128)} %get-tuple-element.468), channel_id=1, source_target_pairs={{0,1},{1,2},{2,3},{3,4},{4,5},{5,6},{6,7},{7,8},{8,9},{9,10},{10,1... | collective-permute-start | bytes 172040 | tf_op jit(solution)/shard_map/while/body/eval_jaxpr/ppermute | solution.py:14
  527.5 18.1 %collective-permute-start = (f32[2,2,4,7,128]{4,3,2,1,0:T(8,128)}, f32[2,2,4,7,128]{4,3,2,1,0:T(8,128)S(1)}, u32[]{:S(2)}, u32[]{:S(2)}) collective-permute-start(f32[2,2,4,7,128]{4,3,2,1,0:T(8,128)} %get-tuple-element.467), channel_id=1, source_target_pairs={{1,0},{2,1},{3,2},{4,3},{5,4},{6,5},{7,6},{8,7},{9,8},{10,9},{11,1... | collective-permute-start | bytes 172040 | tf_op jit(solution)/shard_map/while/body/eval_jaxpr/ppermute | solution.py:15
  529.4 16.2 %collective-permute-start.1 = (f32[2,2,4,7,128]{4,3,2,1,0:T(8,128)}, f32[2,2,4,7,128]{4,3,2,1,0:T(8,128)S(1)}, u32[]{:S(2)}, u32[]{:S(2)}) collective-permute-start(f32[2,2,4,7,128]{4,3,2,1,0:T(8,128)} %get-tuple-element.468), channel_id=1, source_target_pairs={{0,1},{1,2},{2,3},{3,4},{4,5},{5,6},{6,7},{7,8},{8,9},{9,10},{10,1... | collective-permute-start | bytes 172040 | tf_op jit(solution)/shard_map/while/body/eval_jaxpr/ppermute | solution.py:14
  (31 other events, 272.7 us)
where the time goes:
time: 582 us; the launch traced here: 577 us
  starting transfers between devices  230 us (40%)
  other arithmetic  143 us (25%)
  waiting for transfers between devices  90.5 us (16%)
  matrix products  78.3 us (13%)
  local copies, waits for them, and re-layouts  31.1 us (5%)
    ppermute x11, starting transfers between devices, from_behind(): lax.ppermute(value, axis, [(source, source + steps) for source in range(i...  90.6 us
    ppermute x22, starting transfers between devices, padded_2(): after = lax.ppermute(initial, axis, down)  85.1 us
    dot_general x22, matrix products, lookup(): jnp.dot(flat_table, selector, preferred_element_type=jnp.float32, precisi...  78.3 us
    ppermute x22, waiting for transfers between devices, padded_2(): before = lax.ppermute(last, axis, up)  66.7 us
    ppermute x22, starting transfers between devices, padded_2(): before = lax.ppermute(last, axis, up)  54.4 us
    convert_element_type x11, other arithmetic, selector_of(): (lax.broadcasted_iota(jnp.int32, (levels, height * width), 0) == flat_spe...  39.5 us
    mul x132, other arithmetic, chebyshev_sum(): older, newer = (newer, (2.0 * mcclellan(newer) - older) * row_mask)  37.6 us
    ppermute x11, waiting for transfers between devices, from_behind(): lax.ppermute(value, axis, [(source, source + steps) for source in range(i...  23.7 us
  transfers between devices with their start and end apart: 55, of which 22 were waited for; matrix products, arithmetic and copies ran while one was open for 27% of the time, Pallas kernels for 0%

commit v1 on v0

v1 whole, which is shorter than its diff:
```python
import functools

import jax
import jax.numpy as jnp
from jax import lax
from jax.experimental import pallas as pl
from jax.experimental.pallas import tpu as pltpu
from jax.sharding import PartitionSpec as P

MESH = pl.DeviceIdType.MESH
TERMS = 8
BLOCK = 4
TILE = 32
HALO = 32
EXT = 128
PAD = 8
CHUNK = 32


def chebyshev_in_powers():
    rows = [[1], [0, 1]]
    for _ in range(2, TERMS):
        up = [0] + [2 * v for v in rows[-1]]
        old = rows[-2] + [0] * (len(up) - len(rows[-2]))
        rows.append([a - b for a, b in zip(up, old)])
    return rows


def pieces(low, high):
    cuts = {low, high}
    for edge in (24, 32, 96, 104):
        if low < edge < high:
            cuts.add(edge)
    marks = sorted(cuts)
    out = []
    for start, stop in zip(marks[:-1], marks[1:]):
        while start < stop:
            size = min(CHUNK, stop - start)
            out.append((start, size))
            start += size
    return out


def kernel(
    surface, speeds, table, out,
    planes, speed_all, tab, partial, landed, halo,
    local_sem, field_send, field_recv, edge_send, edge_recv,
    gather_send, gather_recv, relay_send, halo_send, halo_recv, image_send, image_recv,
):
    s = lax.axis_index("depth")
    t = lax.axis_index("tile")
    columns = lax.axis_size("tile") // 2
    col, zl = t // 2, t % 2
    zh, core = s // 2, s % 2
    z = zh * 2 + zl
    sibling = zh * 2 + (1 - core)
    outward = jnp.where(zl == 0, t - 1, t + 1)
    beyond = jnp.where(zl == 0, t - 2, t + 2)
    has_out = jnp.where(zl == 0, col > 0, col < columns - 1)
    has_left = col > 0
    has_right = col < columns - 1
    has_in = jnp.where(zl == 0, has_right, has_left)
    inward = jnp.where(zl == 0, t + 2, t - 2)

    def chip(step):
        other = (z + step) % 8
        return other // 2, other % 2

    @pl.when(jnp.logical_not(has_left))
    def _():
        planes[0, :, PAD : PAD + HALO, :] = jnp.zeros((4, HALO, 128), jnp.float32)
        speed_all[:, 0:HALO, :] = jnp.zeros((16, HALO, 128), jnp.int32)

    @pl.when(jnp.logical_not(has_right))
    def _():
        planes[0, :, PAD + EXT - HALO : PAD + EXT, :] = jnp.zeros((4, HALO, 128), jnp.float32)
        speed_all[:, EXT - HALO : EXT, :] = jnp.zeros((16, HALO, 128), jnp.int32)

    barrier = pltpu.get_barrier_semaphore()

    def greet(depth, tile):
        pl.semaphore_signal(barrier, inc=1, device_id=(depth, tile), device_id_type=MESH)

    greet(sibling, t)
    for step in range(1, 8):
        ozh, ozl = chip(step)
        greet(ozh * 2, 2 * col + ozl)
        greet(ozh * 2 + 1, 2 * col + ozl)

    @pl.when(has_out)
    def _():
        greet(s, outward)
        greet(s, beyond)

    @pl.when(has_in)
    def _():
        greet(s, inward)

    freq = s * 2 + zl
    coef = chebyshev_in_powers()
    for part in range(2):
        for power in range(TERMS):
            row = None
            for n in range(power, TERMS):
                c = coef[n][power]
                if c:
                    term = table[freq, part, n : n + 1, :] * (c / 8.0**power)
                    row = term if row is None else row + term
            tab[part * TERMS + power] = jnp.broadcast_to(row, (8, 128))

    pl.semaphore_wait(
        barrier, 15 + 2 * has_out.astype(jnp.int32) + has_in.astype(jnp.int32)
    )

    own_row = HALO + TILE * zl
    far_row = jnp.where(zl == 0, EXT - HALO, 0)

    def edge_copy():
        return pltpu.make_async_remote_copy(
            src_ref=speeds,
            dst_ref=speed_all.at[pl.ds(2 * s, 2), pl.ds(pl.multiple_of(far_row, 32), TILE), :],
            send_sem=edge_send,
            recv_sem=edge_recv,
            device_id=(s, outward),
            device_id_type=MESH,
        )

    @pl.when(has_out)
    def _():
        edge_copy().start()

    own_speed = pltpu.make_async_copy(
        speeds,
        speed_all.at[pl.ds(2 * s, 2), pl.ds(pl.multiple_of(own_row, 32), TILE), :],
        local_sem.at[0],
    )
    own_speed.start()

    def field_copy(target, target_zl, slot, sem):
        wanted = s * 2 + target_zl
        return pltpu.make_async_remote_copy(
            src_ref=surface.at[wanted // 4, :, wanted % 4],
            dst_ref=planes.at[0].at[:, pl.ds(pl.multiple_of(PAD + TILE * slot, 8), TILE), :],
            send_sem=field_send.at[sem],
            recv_sem=field_recv.at[slot],
            device_id=(s, target),
            device_id_type=MESH,
        )

    field_copy(2 * col + 1 - zl, 1 - zl, 1 + zl, 0).start()

    @pl.when(has_out)
    def _():
        slot = jnp.where(zl == 0, 3, 0)
        field_copy(outward, 1 - zl, slot, 1).start()
        field_copy(beyond, zl, slot, 2).start()

    own_field = pltpu.make_async_copy(
        surface.at[freq // 4, :, freq % 4],
        planes.at[0].at[:, pl.ds(pl.multiple_of(PAD + own_row, 8), TILE), :],
        local_sem.at[1],
    )
    own_field.start()

    own_speed.wait()

    @pl.when(has_out)
    def _():
        edge_copy().wait()

    def span(lev, who):
        rows = TILE + 24 - 8 * lev
        return jnp.where(who == 0, HALO + TILE - rows, HALO + TILE), rows

    def level_copy(level, lev, who, target, send):
        first, rows = span(lev, who)
        part = speed_all.at[level, pl.ds(pl.multiple_of(first, 8), rows), :]
        return pltpu.make_async_remote_copy(
            src_ref=part,
            dst_ref=part,
            send_sem=send,
            recv_sem=gather_recv.at[level, who],
            device_id=target,
            device_id_type=MESH,
        )

    for lev in range(2):
        for step in range(1, 8):
            ozh, ozl = chip(step)
            level_copy(
                2 * s + lev, lev, zl, (ozh * 2 + core, 2 * col + ozl), gather_send.at[lev, step]
            ).start()
        level_copy(2 * s + lev, lev, zl, (sibling, t), relay_send.at[lev, 0]).start()
    for step in range(7, 0, -1):
        ozh, ozl = chip(step)
        for lev in range(2):
            level = 2 * (ozh * 2 + core) + lev
            level_copy(level, lev, ozl, (sibling, t), gather_send.at[lev, step]).wait_recv()
            level_copy(level, lev, ozl, (sibling, t), relay_send.at[lev, step]).start()
    for step in range(8):
        ozh, ozl = chip(step)
        for lev in range(2):
            level = 2 * (ozh * 2 + 1 - core) + lev
            level_copy(level, lev, ozl, (sibling, t), relay_send.at[lev, step]).wait_recv()

    own_field.wait()
    field_copy(2 * col + 1 - zl, 1 - zl, 1 + zl, 0).wait_send()
    field_copy(2 * col + 1 - zl, 1 - zl, 2 - zl, 0).wait_recv()

    @pl.when(has_out)
    def _():
        slot = jnp.where(zl == 0, 3, 0)
        field_copy(outward, 1 - zl, slot, 1).wait_send()
        field_copy(beyond, zl, slot, 2).wait_send()

    @pl.when(has_left)
    def _():
        field_copy(t, 1 - zl, 0, 1).wait_recv()

    @pl.when(has_right)
    def _():
        field_copy(t, 1 - zl, 3, 1).wait_recv()

    for lev in range(2):
        for step in range(1, 8):
            level_copy(2 * s + lev, lev, zl, (sibling, t), gather_send.at[lev, step]).wait_send()
        for step in range(8):
            level_copy(2 * s + lev, lev, zl, (sibling, t), relay_send.at[lev, step]).wait_send()

    lane = lax.broadcasted_iota(jnp.int32, (CHUNK, 128), 1)
    first_lane, last_lane = lane == 0, lane == 127
    sub = lax.broadcasted_iota(jnp.int32, (8, 128), 0)
    top_wall = (sub == 7) & jnp.logical_not(has_left)
    low_wall = (sub == 0) & jnp.logical_not(has_right)

    def image_copy(level, half):
        return pltpu.make_async_remote_copy(
            src_ref=partial.at[level, pl.ds(pl.multiple_of(TILE * half, 32), TILE), :],
            dst_ref=landed.at[level % 2, freq],
            send_sem=image_send.at[level, half],
            recv_sem=image_recv.at[level % 2, freq],
            device_id=(level // 2, 2 * col + half),
            device_id_type=MESH,
        )

    def mine(level, half):
        return (level // 2 == s) & (half == zl)

    def halo_copy(block, side):
        return pltpu.make_async_remote_copy(
            src_ref=planes.at[0].at[:, pl.ds(PAD + HALO + TILE * side, TILE), :],
            dst_ref=halo.at[block, 1 - side],
            send_sem=halo_send.at[block, side],
            recv_sem=halo_recv.at[block, 1 - side],
            device_id=(s, t - 2 + 4 * side),
            device_id_type=MESH,
        )

    def run_block(block, carry):
        for lev in range(BLOCK):
            low = 8 * (lev + 1)
            high = EXT - low
            level = block * BLOCK + lev

            def stencil(n, c):
                for p in range(4):
                    for r, size in pieces(low - 8, high + 8):
                        w = planes[n, p, PAD + r : PAD + r + size, :]
                        u = planes[n, p, PAD + r - 1 : PAD + r + size - 1, :]
                        d = planes[n, p, PAD + r + 1 : PAD + r + size + 1, :]
                        x = (u + d) + (w + w)
                        left = jnp.where(first_lane[:size], 0.0, pltpu.roll(x, 1, 1))
                        right = jnp.where(last_lane[:size], 0.0, pltpu.roll(x, 127, 1))
                        g = ((x + x) - 8.0 * w) + (left + right)
                        if r == 24:
                            g = jnp.where(top_wall, 0.0, g)
                        if r == 96:
                            g = jnp.where(low_wall, 0.0, g)
                        planes[n + 1, p, PAD + r : PAD + r + size, :] = g
                return c

            lax.fori_loop(0, TERMS - 1, stencil, 0)
            for r in range(low, high, 8):
                index = speed_all[level, r : r + 8, :]
                total = None
                for n in range(TERMS):
                    cos = jnp.take_along_axis(tab[n], index, axis=1, mode="promise_in_bounds")
                    sin = jnp.take_along_axis(
                        tab[TERMS + n], index, axis=1, mode="promise_in_bounds"
                    )
                    a, b, c, d = (planes[n, p, PAD + r : PAD + r + 8, :] for p in range(4))
                    new = (
                        cos * a - sin * b,
                        cos * b + sin * a,
                        cos * c + sin * d,
                        cos * d - sin * c,
                    )
                    total = new if n == 0 else tuple(o + v for o, v in zip(total, new))
                for p in range(4):
                    planes[0, p, PAD + r : PAD + r + 8, :] = total[p]
                if HALO <= r < EXT - HALO:
                    partial[level, r - HALO : r - HALO + 8, :] = (
                        total[0] * total[2] + total[1] * total[3]
                    )
            for half in range(2):

                @pl.when(jnp.logical_not(mine(level, half)))
                def _():
                    image_copy(level, half).start()

        @pl.when(block < 3)
        def _():
            for side, there in ((0, has_left), (1, has_right)):

                @pl.when(there)
                def _():
                    halo_copy(block, side).start()

            for side, there in ((0, has_left), (1, has_right)):

                @pl.when(there)
                def _():
                    halo_copy(block, side).wait_send()
                    halo_copy(block, 1 - side).wait_recv()
                    base = PAD + (EXT - HALO) * side
                    planes[0, :, base : base + HALO, :] = halo[block, side]

        return carry

    lax.fori_loop(0, 16 // BLOCK, run_block, 0)

    for lev in range(2):
        total = partial[2 * s + lev, pl.ds(pl.multiple_of(TILE * zl, 32), TILE), :]
        for step in range(8):
            ozh, ozl = chip(step)
            for c in range(2):
                if step == 0 and c == 1:
                    continue
                src = (ozh * 2 + (core if c == 0 else 1 - core)) * 2 + ozl
                if step == 0:
                    src = sibling * 2 + zl
                pltpu.make_async_remote_copy(
                    src_ref=partial.at[0, pl.ds(0, TILE), :],
                    dst_ref=landed.at[lev, src],
                    send_sem=image_send.at[0, 0],
                    recv_sem=image_recv.at[lev, src],
                    device_id=(s, t),
                    device_id_type=MESH,
                ).wait_recv()
                total = total + landed[lev, src]
        out[lev] = total

    def drain(level, carry):
        for half in range(2):

            @pl.when(jnp.logical_not(mine(level, half)))
            def _():
                image_copy(level, half).wait_send()

        return carry

    lax.fori_loop(0, 16, drain, 0)


def body(surface, speeds, table):
    vmem = pl.BlockSpec(memory_space=pltpu.VMEM)
    dma = pltpu.SemaphoreType.DMA
    return pl.pallas_call(
        kernel,
        out_shape=jax.ShapeDtypeStruct((2, TILE, 128), jnp.float32),
        in_specs=[pl.BlockSpec(memory_space=pl.ANY), vmem, vmem],
        out_specs=vmem,
        scratch_shapes=[
            pltpu.VMEM((TERMS, 4, EXT + 2 * PAD, 128), jnp.float32),
            pltpu.VMEM((16, EXT, 128), jnp.int32),
            pltpu.VMEM((2 * TERMS, 8, 128), jnp.float32),
            pltpu.VMEM((16, 2 * TILE, 128), jnp.float32),
            pltpu.VMEM((2, 16, TILE, 128), jnp.float32),
            pltpu.VMEM((3, 2, 4, HALO, 128), jnp.float32),
            dma((2,)),
            dma((3,)),
            dma((4,)),
            dma,
            dma,
            dma((2, 8)),
            dma((16, 2)),
            dma((2, 8)),
            dma((3, 2)),
            dma((3, 2)),
            dma((16, 2)),
            dma((2, 16)),
        ],
        compiler_params=pltpu.CompilerParams(
            collective_id=0, has_side_effects=True, vmem_limit_bytes=32 << 20
        ),
    )(surface, speeds, table)


def solution(mesh):
    def flat(surface, speeds, table):
        return body(surface.reshape(4, 4, 4, TILE, 128), speeds, table)

    return jax.shard_map(
        flat,
        mesh=mesh,
        in_specs=(P(None, None, None, None, "tile", None), P("depth", "tile", None), P()),
        out_specs=P("depth", "tile", None),
        check_vma=False,
    )
```

time: 582 us -> 71 us (0.12)
  the two profiles are of different devices: /device:TPU:89 before, /device:TPU:6 now
where the time goes in v1:
time: 71 us; the launch traced here: 69.7 us
  Pallas kernels  66.2 us (93%)
  local copies, waits for them, and re-layouts  3.5 us (5%)
    pallas_call x1, Pallas kernels, body(): pl.pallas_call(kernel, out_shape=jax.ShapeDtypeStruct((2, TILE, 128), jnp...  66.2 us
    unnamed x7, local copies, waits for them, and re-layouts  3.5 us

profile of v1, /device:TPU:6, one launch (start us, length us, event | category | flops | bytes accessed | tf_op | source)
XLA Modules:
  0.0 69.7 jit_solution(5520025569496722213)
XLA Ops:
  0.0 0.0 copy-start
  0.0 1.2 %copy-done = f32[4,2,2,4,32,128]{5,4,3,2,1,0:T(8,128)S(1)} copy-done((f32[4,2,2,4,32,128]{5,4,3,2,1,0:T(8,128)S(1)}, f32[4,2,2,4,32,128]{5,4,3,2,1,0:T(8,128)}, u32[]{:S(2)}) %copy-start) | copy-done | bytes 1048600
  1.2 0.0 copy-start.1
  1.2 0.9 %copy-done.1 = f32[16,2,8,128]{3,2,1,0:T(8,128)S(1)} copy-done((f32[16,2,8,128]{3,2,1,0:T(8,128)S(1)}, f32[16,2,8,128]{3,2,1,0:T(8,128)}, u32[]{:S(2)}) %copy-start.1) | copy-done | bytes 131096
  2.1 0.0 copy-start.2
  2.1 0.8 %copy-done.2 = s32[2,32,128]{2,1,0:T(8,128)S(1)} copy-done((s32[2,32,128]{2,1,0:T(8,128)S(1)}, s32[2,32,128]{2,1,0:T(8,128)}, u32[]{:S(2)}) %copy-start.2) | copy-done | bytes 32792
  2.9 66.2 %shard_map.37 = f32[2,32,128]{2,1,0:T(8,128)S(1)} custom-call(f32[4,4,4,32,128]{4,3,2,1,0:T(8,128)S(1)} %bitcast.1, s32[2,32,128]{2,1,0:T(8,128)S(1)} %copy-done.2, f32[16,2,8,128]{3,2,1,0:T(8,128)S(1)} %copy-done.1), custom_call_target="tpu_custom_call" | custom-call | tf_op jit(solution)/shard_map/pallas_call | solution.py:368
  69.1 0.6 copy.5
Async XLA Ops:
  0.0 1.2 %copy-start = (f32[4,2,2,4,32,128]{5,4,3,2,1,0:T(8,128)S(1)}, f32[4,2,2,4,32,128]{5,4,3,2,1,0:T(8,128)}, u32[]{:S(2)}) copy-start(f32[4,2,2,4,32,128]{5,4,3,2,1,0:T(8,128)} %param.3) | copy-start | bytes 3145732
  1.2 0.9 %copy-start.1 = (f32[16,2,8,128]{3,2,1,0:T(8,128)S(1)}, f32[16,2,8,128]{3,2,1,0:T(8,128)}, u32[]{:S(2)}) copy-start(f32[16,2,8,128]{3,2,1,0:T(8,128)} %table.1) | copy-start | bytes 393220
  2.1 0.8 %copy-start.2 = (s32[2,32,128]{2,1,0:T(8,128)S(1)}, s32[2,32,128]{2,1,0:T(8,128)}, u32[]{:S(2)}) copy-start(s32[2,32,128]{2,1,0:T(8,128)} %speeds.1) | copy-start | bytes 98308

commit v2 on v0

v2 whole, which is shorter than its diff:
```python
import jax
import jax.numpy as jnp
from jax import lax
from jax.experimental import pallas as pl
from jax.experimental.pallas import tpu as pltpu
from jax.sharding import PartitionSpec as P

MESH = pl.DeviceIdType.MESH
TERMS = 8
LEVELS = 16
PLACES = 8
TILE = 32
FOLD = 96
OWN = 64
EXT = 192
MIRROR = 104
PAD = 8


def chebyshev_in_powers():
    rows = [[1], [0, 1]]
    for _ in range(2, TERMS):
        up = [0] + [2 * v for v in rows[-1]]
        old = rows[-2] + [0] * (len(up) - len(rows[-2]))
        rows.append([a - b for a, b in zip(up, old)])
    return rows


def spans(low, high):
    marks = [low] + [m for m in (16, 32, 56, 64, 80) if m > low] + [high]
    return [(start, stop - start) for start, stop in zip(marks[:-1], marks[1:])]


def kernel(
    surface, speeds, table, out,
    field, stage, planes, raw, speed, rim, table_row, tab, indices,
    partial, beside, joined, landed, halo,
    local_sem, field_send, field_recv, speed_send, speed_recv, relay_send, rim_send, rim_recv,
    halo_send, halo_recv, beside_send, beside_recv, image_send, image_recv,
):
    s = lax.axis_index("depth")
    t = lax.axis_index("tile")
    columns = lax.axis_size("tile") // 2
    col, zl = t // 2, t % 2
    zh, core = s // 2, s % 2
    z = zh * 2 + zl
    freq = s * 2 + zl
    sibling = zh * 2 + (1 - core)
    has_left = col > 0
    has_right = col < columns - 1
    sides = ((0, has_left), (1, has_right))

    def chip(step):
        other = (z + step) % 8
        return other // 2, other % 2

    def rows(first, size):
        return pl.ds(pl.multiple_of(first, 8), size)

    lane = lax.broadcasted_iota(jnp.int32, (8, 128), 1)
    sub = lax.broadcasted_iota(jnp.int32, (8, 128), 0)
    low_half = lane < 64
    bit0, bit1 = sub % 2 == 0, (sub // 2) % 2 == 0
    parity = jnp.where(low_half, 2 * lane, 2 * lane - 127)
    interleave = lane // 2 + 64 * (lane % 2)
    wall = (sub == 7) & (
        (low_half & jnp.logical_not(has_left))
        | (jnp.logical_not(low_half) & jnp.logical_not(has_right))
    )
    tall = lax.broadcasted_iota(jnp.int32, (24, 128), 1) % 64
    first_lane, last_lane = tall == 0, tall == 63

    def swap(v):
        return pltpu.roll(v, 64, 1)

    def reverse(v):
        v = pltpu.roll(v, 4, 0)
        v = jnp.where(bit1, pltpu.roll(v, 6, 0), pltpu.roll(v, 2, 0))
        return jnp.where(bit0, pltpu.roll(v, 7, 0), pltpu.roll(v, 1, 0))

    def split(v):
        return jnp.take_along_axis(v, parity, axis=1, mode="promise_in_bounds")

    def join(top, low):
        return jnp.where(low_half, top, swap(low)), jnp.where(low_half, swap(top), low)

    def mirror(p, eo, v):
        planes[0, p, eo, PAD + FOLD : PAD + MIRROR, :] = reverse(swap(v))

    other_freq = s * 2 + 1 - zl
    local = (
        pltpu.make_async_copy(speeds, raw, local_sem.at[0]),
        pltpu.make_async_copy(
            surface.at[freq // 4, :, freq % 4],
            field.at[:, rows(OWN + TILE * zl, TILE), :],
            local_sem.at[1],
        ),
        pltpu.make_async_copy(
            surface.at[other_freq // 4, :, other_freq % 4], stage, local_sem.at[2]
        ),
        pltpu.make_async_copy(table.at[freq], table_row, local_sem.at[3]),
    )
    for copy in local:
        copy.start()

    for side, there in sides:

        @pl.when(jnp.logical_not(there))
        def _():
            base = 2 * OWN * side
            field[:, base : base + OWN, :] = jnp.zeros((4, OWN, 128), jnp.float32)
            rim[:, side] = jnp.zeros((LEVELS, 2, TILE, 128), jnp.int32)
            halo[side] = jnp.zeros((4, 2, TILE, 128), jnp.float32)

    barrier = pltpu.get_barrier_semaphore()

    def greet(depth, tile):
        pl.semaphore_signal(barrier, inc=1, device_id=(depth, tile), device_id_type=MESH)

    for step in range(4, 12):
        ozh, ozl = chip(step)
        if step != 8:
            greet(ozh * 2, 2 * col + ozl)
            greet(ozh * 2 + 1, 2 * col + ozl)

    for side, there in sides:

        @pl.when(there)
        def _():
            greet(s, 2 * (col - 1 + 2 * side))
            greet(s, 2 * (col - 1 + 2 * side) + 1)

    greet(sibling, t)

    for copy in local:
        copy.wait()

    coef = chebyshev_in_powers()
    for part in range(2):
        for power in range(TERMS):
            row = None
            for n in range(power, TERMS):
                c = coef[n][power]
                if c:
                    term = table_row[part, n : n + 1, :] * (c / 8.0**power)
                    row = term if row is None else row + term
            tab[part * TERMS + power] = jnp.broadcast_to(row, (8, 128))

    for lev in range(2):
        for r in range(0, TILE, 8):
            straight = split(raw[lev, r : r + 8, :])
            turned = reverse(split(raw[lev, 24 - r : TILE - r, :]))
            speed[2 * s + lev, zl, r : r + 8, :] = jnp.where(zl == 0, straight, turned)

    pl.semaphore_wait(
        barrier, 15 + 2 * has_left.astype(jnp.int32) + 2 * has_right.astype(jnp.int32)
    )

    def speed_copy(owner, owner_zl, target, sem):
        part = speed.at[pl.ds(2 * owner, 2), owner_zl]
        return pltpu.make_async_remote_copy(
            src_ref=part,
            dst_ref=part,
            send_sem=sem,
            recv_sem=speed_recv.at[owner, owner_zl],
            device_id=target,
            device_id_type=MESH,
        )

    def each_speed(action):
        for step in (4, 3, 5, 2, 6, 1, 7):
            ozh, ozl = chip(step)
            action(
                speed_copy(s, zl, (ozh * 2 + core, 2 * col + ozl), speed_send.at[step])
            )
        action(speed_copy(s, zl, (sibling, t), speed_send.at[0]))

    def relay(owner, owner_zl):
        return speed_copy(owner, owner_zl, (sibling, t), relay_send.at[owner // 2, owner_zl])

    def foreign(owner, owner_zl):
        return jnp.logical_not((owner == s) & (owner_zl == zl))

    def passes(owner, owner_zl):
        return foreign(owner, owner_zl) & (owner % 2 == core)

    def take_speeds(first, last):
        for owner in range(first, last):
            for owner_zl in range(2):

                @pl.when(passes(owner, owner_zl))
                def _():
                    relay(owner, owner_zl).wait_recv()
                    relay(owner, owner_zl).start()

        for owner in range(first, last):
            for owner_zl in range(2):

                @pl.when(owner % 2 != core)
                def _():
                    relay(owner, owner_zl).wait_recv()

    def start(copy):
        copy.start()

    def wait_send(copy):
        copy.wait_send()

    @pl.when(s == 0)
    def _():
        each_speed(start)

    def field_copy(source, target, row, sem):
        return pltpu.make_async_remote_copy(
            src_ref=source,
            dst_ref=field.at[:, rows(row, TILE), :],
            send_sem=field_send.at[sem],
            recv_sem=field_recv.at[row // TILE],
            device_id=(s, target),
            device_id_type=MESH,
        )

    own_field = field.at[:, rows(OWN + TILE * zl, TILE), :]
    inner = field_copy(stage, 2 * col + 1 - zl, OWN + TILE * zl, 0)

    def outer(side):
        target = 2 * (col - 1 + 2 * side)
        row = 2 * OWN * (1 - side) + TILE * zl
        return (
            field_copy(stage, target + 1 - zl, row, 1 + 2 * side),
            field_copy(own_field, target + zl, row, 2 + 2 * side),
        )

    inner.start()
    for side, there in sides:

        @pl.when(there)
        def _():
            for copy in outer(side):
                copy.start()

    field_copy(stage, t, OWN + TILE * (1 - zl), 0).wait_recv()
    for side, there in sides:

        @pl.when(there)
        def _():
            for part in range(2):
                field_copy(stage, t, 2 * OWN * side + TILE * part, 0).wait_recv()

    inner.wait_send()
    for side, there in sides:

        @pl.when(there)
        def _():
            for copy in outer(side):
                copy.wait_send()

    @pl.when(s > 0)
    def _():
        each_speed(start)

    def fold_plane(p, c):
        sign = jnp.where(p == 3, -1.0, 1.0)
        tops = [split(field[p, r : r + 8, :] * sign) for r in range(0, FOLD, 8)]
        lows = [split(reverse(field[p, EXT - 8 - r : EXT - r, :] * sign)) for r in range(0, FOLD, 8)]
        for j in range(FOLD // 8):
            for eo, v in enumerate(join(tops[j], lows[j])):
                planes[0, p, eo, PAD + 8 * j : PAD + 8 * j + 8, :] = v
                if j == FOLD // 8 - 1:
                    mirror(p, eo, v)
        return c

    lax.fori_loop(0, 4, fold_plane, 0)

    def velocity(level, r):
        if r >= OWN:
            at = r - OWN
            return join(speed[level, 0, at : at + 8, :], speed[level, 1, at : at + 8, :])
        if r >= TILE:
            at = OWN - 8 - r
            return join(
                reverse(rim[level, 0, 1, at : at + 8, :]),
                reverse(rim[level, 1, 0, at : at + 8, :]),
            )
        return join(rim[level, 0, 0, r : r + 8, :], rim[level, 1, 1, r : r + 8, :])

    def rim_copy(turn, place, side):
        level = PLACES * turn + place
        size = 8 * (7 - place)
        if size > TILE:
            source, target = speed.at[level], rim.at[level, 1 - side]
        else:
            source = speed.at[level, side, pl.ds(0, size), :]
            target = rim.at[level, 1 - side, side, pl.ds(0, size), :]
        return pltpu.make_async_remote_copy(
            src_ref=source,
            dst_ref=target,
            send_sem=rim_send.at[turn, place, side],
            recv_sem=rim_recv.at[turn, place, 1 - side],
            device_id=(s, t - 2 + 4 * side),
            device_id_type=MESH,
        )

    def each_rim(turn, places, action):
        for place in places:
            for side, there in sides:

                @pl.when(there)
                def _():
                    action(rim_copy(turn, place, side))

    def halo_copy(side):
        return pltpu.make_async_remote_copy(
            src_ref=planes.at[0].at[:, :, pl.ds(PAD + OWN, TILE), :],
            dst_ref=halo.at[1 - side],
            send_sem=halo_send.at[side],
            recv_sem=halo_recv.at[1 - side],
            device_id=(s, t - 2 + 4 * side),
            device_id_type=MESH,
        )

    def send_halo():
        for side, there in sides:

            @pl.when(there)
            def _():
                halo_copy(side).start()

    def take_halo():
        for side, there in sides:

            @pl.when(there)
            def _():
                halo_copy(1 - side).wait_recv()
                halo_copy(side).wait_send()

        def place_plane(p, c):
            for eo in range(2):
                for r in range(0, TILE, 8):
                    left = halo[0, p, eo, r : r + 8, :]
                    right = halo[1, p, eo, r : r + 8, :]
                    planes[0, p, eo, PAD + r : PAD + r + 8, :] = jnp.where(low_half, left, right)
                    far = PAD + OWN - 8 - r
                    planes[0, p, eo, far : far + 8, :] = reverse(
                        swap(jnp.where(low_half, right, left))
                    )
            return c

        lax.fori_loop(0, 4, place_plane, 0)

    def stencil(n, low, high):
        for p in range(4):
            for r, size in spans(low, high):
                at = PAD + r
                near, far = [], []
                for eo in range(2):
                    w = planes[n, p, eo, at : at + size, :]
                    ring = planes[n, p, eo, at - 1 : at + size - 1, :] + (
                        planes[n, p, eo, at + 1 : at + size + 1, :]
                    )
                    near.append(ring + (w + w))
                    far.append(ring - (w + w))
                left = jnp.where(first_lane[:size], 0.0, pltpu.roll(near[1], 1, 1))
                right = jnp.where(last_lane[:size], 0.0, pltpu.roll(near[0], 127, 1))
                both = (
                    (far[0] + far[0]) + (near[1] + left),
                    (far[1] + far[1]) + (near[0] + right),
                )
                for eo, g in enumerate(both):
                    if r == 56:
                        g = jnp.where(wall, 0.0, g)
                    planes[n + 1, p, eo, at : at + size, :] = g

    def beside_copy(level):
        return pltpu.make_async_remote_copy(
            src_ref=partial.at[level, 1 - core],
            dst_ref=beside.at[level],
            send_sem=beside_send.at[level],
            recv_sem=beside_recv.at[level],
            device_id=(sibling, t),
            device_id_type=MESH,
        )

    def image_copy(level):
        return pltpu.make_async_remote_copy(
            src_ref=joined.at[level],
            dst_ref=landed.at[level % 2, z],
            send_sem=image_send.at[level],
            recv_sem=image_recv.at[level % 2, z],
            device_id=(level // 2, 2 * col + core),
            device_id_type=MESH,
        )

    def mine(level):
        return (level // 2 == s) & (core == zl)

    def pass_on(level):
        beside_copy(level).wait_recv()
        total = partial[level, core] + beside[level]

        @pl.when(mine(level))
        def _():
            landed[level % 2, z] = total

        @pl.when(jnp.logical_not(mine(level)))
        def _():
            joined[level] = total
            image_copy(level).start()

    def advance(turn, place):
        low = 8 * (place + 1)
        level = PLACES * turn + place

        def find_indices():
            if place < PLACES - 1:
                for side, there in sides:

                    @pl.when(there)
                    def _():
                        rim_copy(turn, place, 1 - side).wait_recv()

            for r in range(low, FOLD, 8):
                for eo, index in enumerate(velocity(level, r)):
                    indices[eo, r : r + 8, :] = index

        if place:
            find_indices()
        for n in range(TERMS - 2):
            stencil(n, low - 8, MIRROR)
        stencil(TERMS - 2, low, FOLD)
        if not place:
            find_indices()
        for r in range(FOLD - 8, low - 8, -8):
            image = []
            for eo in range(2):
                index = indices[eo, r : r + 8, :]
                total = None
                for n in range(TERMS):
                    cos = jnp.take_along_axis(tab[n], index, axis=1, mode="promise_in_bounds")
                    sin = jnp.take_along_axis(
                        tab[TERMS + n], index, axis=1, mode="promise_in_bounds"
                    )
                    a, b, c, d = (planes[n, p, eo, PAD + r : PAD + r + 8, :] for p in range(4))
                    new = (
                        cos * a - sin * b,
                        cos * b + sin * a,
                        cos * c - sin * d,
                        cos * d + sin * c,
                    )
                    total = new if n == 0 else tuple(o + v for o, v in zip(total, new))
                for p in range(4):
                    planes[0, p, eo, PAD + r : PAD + r + 8, :] = total[p]
                    if r == FOLD - 8:
                        mirror(p, eo, total[p])
                image.append(total[0] * total[2] - total[1] * total[3])
            if r >= OWN:
                for half, v in enumerate(join(image[0], image[1])):
                    partial[level, half, r - OWN : r - OWN + 8, :] = v
        beside_copy(level).start()

        @pl.when(level > 0)
        def _():
            pass_on(level - 1)

    def run_turn(turn, carry):
        @pl.when(turn == 0)
        def _():
            take_speeds(0, 1)
            each_rim(0, (0, 1), start)
            for owner in range(1, 4):
                take_speeds(owner, owner + 1)
                each_rim(0, (2 * owner, 2 * owner + 1)[: 7 - 2 * owner], start)

        @pl.when(turn == 1)
        def _():
            send_halo()
            take_halo()

        for place in range(PLACES):
            advance(turn, place)
            if place == 3:

                @pl.when(turn == 0)
                def _():
                    take_speeds(4, 8)
                    each_rim(1, range(7), start)

        return carry

    lax.fori_loop(0, 2, run_turn, 0)
    pass_on(LEVELS - 1)

    for lev in range(2):
        for step in (0, 1, 7, 2, 6, 3, 5, 4):
            source = (z + step) % 8
            arrival = pltpu.make_async_remote_copy(
                src_ref=joined.at[0],
                dst_ref=landed.at[lev, source],
                send_sem=image_send.at[0],
                recv_sem=image_recv.at[lev, source],
                device_id=(s, t),
                device_id_type=MESH,
            )
            if step:
                arrival.wait_recv()
            else:

                @pl.when(core != zl)
                def _():
                    arrival.wait_recv()

        sums = []
        for r in range(0, TILE, 8):
            total = landed[lev, 0, r : r + 8, :]
            for source in range(1, 8):
                total = total + landed[lev, source, r : r + 8, :]
            sums.append(jnp.take_along_axis(total, interleave, axis=1, mode="promise_in_bounds"))
        for j in range(4):
            out[lev, 8 * j : 8 * j + 8, :] = jnp.where(zl == 0, sums[j], reverse(sums[3 - j]))

    each_speed(wait_send)
    for owner in range(8):
        for owner_zl in range(2):

            @pl.when(passes(owner, owner_zl))
            def _():
                relay(owner, owner_zl).wait_send()

    for turn in range(2):
        each_rim(turn, range(7), wait_send)

    def drain(level, carry):
        beside_copy(level).wait_send()

        @pl.when(jnp.logical_not(mine(level)))
        def _():
            image_copy(level).wait_send()

        return carry

    lax.fori_loop(0, LEVELS, drain, 0)


def body(surface, speeds, table):
    hbm = pl.BlockSpec(memory_space=pltpu.HBM)
    dma = pltpu.SemaphoreType.DMA

    def vmem(*shape, dtype=jnp.float32):
        return pltpu.VMEM(shape, dtype)

    return pl.pallas_call(
        kernel,
        out_shape=jax.ShapeDtypeStruct((2, TILE, 128), jnp.float32),
        in_specs=[hbm, hbm, hbm],
        out_specs=pl.BlockSpec(memory_space=pltpu.VMEM),
        scratch_shapes=[
            vmem(4, EXT, 128),
            vmem(4, TILE, 128),
            vmem(TERMS, 4, 2, MIRROR + 2 * PAD, 128),
            vmem(2, TILE, 128, dtype=jnp.int32),
            vmem(LEVELS, 2, TILE, 128, dtype=jnp.int32),
            vmem(LEVELS, 2, 2, TILE, 128, dtype=jnp.int32),
            vmem(2, TERMS, 128),
            vmem(2 * TERMS, 8, 128),
            vmem(2, FOLD, 128, dtype=jnp.int32),
            vmem(LEVELS, 2, TILE, 128),
            vmem(LEVELS, TILE, 128),
            vmem(LEVELS, TILE, 128),
            vmem(2, 8, TILE, 128),
            vmem(2, 4, 2, TILE, 128),
            dma((4,)),
            dma((5,)),
            dma((6,)),
            dma((8,)),
            dma((8, 2)),
            dma((4, 2)),
            dma((2, 7, 2)),
            dma((2, 7, 2)),
            dma((2,)),
            dma((2,)),
            dma((LEVELS,)),
            dma((LEVELS,)),
            dma((LEVELS,)),
            dma((2, 8)),
        ],
        compiler_params=pltpu.CompilerParams(
            collective_id=0, has_side_effects=True, vmem_limit_bytes=60 << 20
        ),
    )(surface, speeds, table)


def solution(mesh):
    def flat(surface, speeds, table):
        return body(surface.reshape(4, 4, 4, TILE, 128), speeds, table)

    return jax.shard_map(
        flat,
        mesh=mesh,
        in_specs=(P(None, None, None, None, "tile", None), P("depth", "tile", None), P()),
        out_specs=P("depth", "tile", None),
        check_vma=False,
    )
```

time: 582 us -> 61.4 us (0.11)
  the two profiles are of different devices: /device:TPU:89 before, /device:TPU:6 now
where the time goes in v2:
time: 61.4 us; the launch traced here: 61.3 us
  Pallas kernels  59.9 us (98%)
  local copies, waits for them, and re-layouts  1.38 us (2%)
    pallas_call x1, Pallas kernels, body(): pl.pallas_call(kernel, out_shape=jax.ShapeDtypeStruct((2, TILE, 128), jnp...  59.9 us
    unnamed x1, local copies, waits for them, and re-layouts  1.38 us

profile of v2, /device:TPU:6, one launch (start us, length us, event | category | flops | bytes accessed | tf_op | source)
XLA Modules:
  0.0 61.3 jit_solution(6583393396107208656)
XLA Ops:
  0.0 59.9 %shard_map.37 = f32[2,32,128]{2,1,0:T(8,128)} custom-call(f32[4,4,4,32,128]{4,3,2,1,0:T(8,128)} %bitcast.1, s32[2,32,128]{2,1,0:T(8,128)} %speeds.1, f32[16,2,8,128]{3,2,1,0:T(8,128)} %table.1), custom_call_target="tpu_custom_call" | custom-call | tf_op jit(solution)/shard_map/pallas_call | solution.py:551
  59.9 1.4 %copy.5 = f32[2,32,128]{2,1,0:T(8,128)} copy(f32[2,32,128]{2,1,0:T(8,128)} %shard_map.37) | data formatting | bytes 65536

commit v3 on v2

--- a/solution.py
+++ b/solution.py
@@ -27,13 +27,13 @@
 
 
 def spans(low, high):
-    marks = [low] + [m for m in (16, 32, 56, 64, 80) if m > low] + [high]
+    marks = [low] + [m for m in (16, 32, 56, 64, 80) if low < m < high] + [high]
     return [(start, stop - start) for start, stop in zip(marks[:-1], marks[1:])]
 
 
 def kernel(
     surface, speeds, table, out,
-    field, stage, planes, raw, speed, rim, table_row, tab, indices,
+    field, stage, planes, raw, speed, rim, table_row, tab, factors,
     partial, beside, joined, landed, halo,
     local_sem, field_send, field_recv, speed_send, speed_recv, relay_send, rim_send, rim_recv,
     halo_send, halo_recv, beside_send, beside_recv, image_send, image_recv,
@@ -206,7 +206,7 @@
     def wait_send(copy):
         copy.wait_send()
 
-    @pl.when(s == 0)
+    @pl.when(s < 2)
     def _():
         each_speed(start)
 
@@ -238,51 +238,6 @@
         def _():
             for copy in outer(side):
                 copy.start()
-
-    field_copy(stage, t, OWN + TILE * (1 - zl), 0).wait_recv()
-    for side, there in sides:
-
-        @pl.when(there)
-        def _():
-            for part in range(2):
-                field_copy(stage, t, 2 * OWN * side + TILE * part, 0).wait_recv()
-
-    inner.wait_send()
-    for side, there in sides:
-
-        @pl.when(there)
-        def _():
-            for copy in outer(side):
-                copy.wait_send()
-
-    @pl.when(s > 0)
-    def _():
-        each_speed(start)
-
-    def fold_plane(p, c):
-        sign = jnp.where(p == 3, -1.0, 1.0)
-        tops = [split(field[p, r : r + 8, :] * sign) for r in range(0, FOLD, 8)]
-        lows = [split(reverse(field[p, EXT - 8 - r : EXT - r, :] * sign)) for r in range(0, FOLD, 8)]
-        for j in range(FOLD // 8):
-            for eo, v in enumerate(join(tops[j], lows[j])):
-                planes[0, p, eo, PAD + 8 * j : PAD + 8 * j + 8, :] = v
-                if j == FOLD // 8 - 1:
-                    mirror(p, eo, v)
-        return c
-
-    lax.fori_loop(0, 4, fold_plane, 0)
-
-    def velocity(level, r):
-        if r >= OWN:
-            at = r - OWN
-            return join(speed[level, 0, at : at + 8, :], speed[level, 1, at : at + 8, :])
-        if r >= TILE:
-            at = OWN - 8 - r
-            return join(
-                reverse(rim[level, 0, 1, at : at + 8, :]),
-                reverse(rim[level, 1, 0, at : at + 8, :]),
-            )
-        return join(rim[level, 0, 0, r : r + 8, :], rim[level, 1, 1, r : r + 8, :])
 
     def rim_copy(turn, place, side):
         level = PLACES * turn + place
@@ -309,6 +264,51 @@
                 def _():
                     action(rim_copy(turn, place, side))
 
+    take_speeds(0, 1)
+    each_rim(0, (0, 1), start)
+
+    @pl.when((s > 1) & (s < 4))
+    def _():
+        each_speed(start)
+
+    field_copy(stage, t, OWN + TILE * (1 - zl), 0).wait_recv()
+    for side, there in sides:
+
+        @pl.when(there)
+        def _():
+            for part in range(2):
+                field_copy(stage, t, 2 * OWN * side + TILE * part, 0).wait_recv()
+
+    inner.wait_send()
+    for side, there in sides:
+
+        @pl.when(there)
+        def _():
+            for copy in outer(side):
+                copy.wait_send()
+
+    for p in range(4):
+        sign = -1.0 if p == 3 else 1.0
+        tops = [split(field[p, r : r + 8, :] * sign) for r in range(0, FOLD, 8)]
+        lows = [split(reverse(field[p, EXT - 8 - r : EXT - r, :] * sign)) for r in range(0, FOLD, 8)]
+        for j in range(FOLD // 8):
+            for eo, v in enumerate(join(tops[j], lows[j])):
+                planes[0, p, eo, PAD + 8 * j : PAD + 8 * j + 8, :] = v
+                if j == FOLD // 8 - 1:
+                    mirror(p, eo, v)
+
+    def velocity(level, r):
+        if r >= OWN:
+            at = r - OWN
+            return join(speed[level, 0, at : at + 8, :], speed[level, 1, at : at + 8, :])
+        if r >= TILE:
+            at = OWN - 8 - r
+            return join(
+                reverse(rim[level, 0, 1, at : at + 8, :]),
+                reverse(rim[level, 1, 0, at : at + 8, :]),
+            )
+        return join(rim[level, 0, 0, r : r + 8, :], rim[level, 1, 1, r : r + 8, :])
+
     def halo_copy(side):
         return pltpu.make_async_remote_copy(
             src_ref=planes.at[0].at[:, :, pl.ds(PAD + OWN, TILE), :],
@@ -334,22 +334,20 @@
                 halo_copy(1 - side).wait_recv()
                 halo_copy(side).wait_send()
 
-        def place_plane(p, c):
+        for p in range(4):
             for eo in range(2):
+                far = []
                 for r in range(0, TILE, 8):
                     left = halo[0, p, eo, r : r + 8, :]
                     right = halo[1, p, eo, r : r + 8, :]
                     planes[0, p, eo, PAD + r : PAD + r + 8, :] = jnp.where(low_half, left, right)
-                    far = PAD + OWN - 8 - r
-                    planes[0, p, eo, far : far + 8, :] = reverse(
-                        swap(jnp.where(low_half, right, left))
-                    )
-            return c
-
-        lax.fori_loop(0, 4, place_plane, 0)
+                    far.append(swap(jnp.where(low_half, right, left)))
+                for j, v in enumerate(far):
+                    at = PAD + OWN - 8 - 8 * j
+                    planes[0, p, eo, at : at + 8, :] = reverse(v)
 
     def stencil(n, low, high):
-        for p in range(4):
+        for p in (slice(0, 2), slice(2, 4)):
             for r, size in spans(low, high):
                 at = PAD + r
                 near, far = [], []
@@ -360,8 +358,8 @@
                     )
                     near.append(ring + (w + w))
                     far.append(ring - (w + w))
-                left = jnp.where(first_lane[:size], 0.0, pltpu.roll(near[1], 1, 1))
-                right = jnp.where(last_lane[:size], 0.0, pltpu.roll(near[0], 127, 1))
+                left = jnp.where(first_lane[:size], 0.0, pltpu.roll(near[1], 1, 2))
+                right = jnp.where(last_lane[:size], 0.0, pltpu.roll(near[0], 127, 2))
                 both = (
                     (far[0] + far[0]) + (near[1] + left),
                     (far[1] + far[1]) + (near[0] + right),
@@ -407,47 +405,61 @@
             joined[level] = total
             image_copy(level).start()
 
+    def find_factors(turn, place):
+        if place < PLACES - 1:
+            for side, there in sides:
+
+                @pl.when(there)
+                def _():
+                    rim_copy(turn, place, 1 - side).wait_recv()
+
+        span = range(8 * (place + 1), FOLD, 8)
+        pairs = [velocity(PLACES * turn + place, r) for r in span]
+        for r, pair in zip(span, pairs):
+            for eo in range(2):
+                at = 2 * r + 8 * eo
+                for n in range(2 * TERMS):
+                    factors[place, n, at : at + 8, :] = jnp.take_along_axis(
+                        tab[n], pair[eo], axis=1, mode="promise_in_bounds"
+                    )
+
     def advance(turn, place):
         low = 8 * (place + 1)
         level = PLACES * turn + place
 
-        def find_indices():
-            if place < PLACES - 1:
-                for side, there in sides:
-
-                    @pl.when(there)
-                    def _():
-                        rim_copy(turn, place, 1 - side).wait_recv()
-
-            for r in range(low, FOLD, 8):
-                for eo, index in enumerate(velocity(level, r)):
-                    indices[eo, r : r + 8, :] = index
-
-        if place:
-            find_indices()
         for n in range(TERMS - 2):
             stencil(n, low - 8, MIRROR)
         stencil(TERMS - 2, low, FOLD)
-        if not place:
-            find_indices()
+
+        @pl.when(turn == 0)
+        def _():
+            if not place:
+                take_speeds(1, 2)
+                each_rim(0, (2, 3), start)
+
+                @pl.when(s >= 4)
+                def _():
+                    each_speed(start)
+
+            find_factors(turn, place)
+
         for r in range(FOLD - 8, low - 8, -8):
             image = []
             for eo in range(2):
-                index = indices[eo, r : r + 8, :]
-                total = None
+                by_cos = by_sin = None
+                at = 2 * r + 8 * eo
                 for n in range(TERMS):
-                    cos = jnp.take_along_axis(tab[n], index, axis=1, mode="promise_in_bounds")
-                    sin = jnp.take_along_axis(
-                        tab[TERMS + n], index, axis=1, mode="promise_in_bounds"
-                    )
-                    a, b, c, d = (planes[n, p, eo, PAD + r : PAD + r + 8, :] for p in range(4))
-                    new = (
-                        cos * a - sin * b,
-                        cos * b + sin * a,
-                        cos * c - sin * d,
-                        cos * d + sin * c,
-                    )
-                    total = new if n == 0 else tuple(o + v for o, v in zip(total, new))
+                    term = planes[n, :, eo, PAD + r : PAD + r + 8, :]
+                    cos = factors[place, n, at : at + 8, :] * term
+                    sin = factors[place, TERMS + n, at : at + 8, :] * term
+                    by_cos = cos if n == 0 else by_cos + cos
+                    by_sin = sin if n == 0 else by_sin + sin
+                total = (
+                    by_cos[0] - by_sin[1],
+                    by_cos[1] + by_sin[0],
+                    by_cos[2] - by_sin[3],
+                    by_cos[3] + by_sin[2],
+                )
                 for p in range(4):
                     planes[0, p, eo, PAD + r : PAD + r + 8, :] = total[p]
                     if r == FOLD - 8:
@@ -456,6 +468,12 @@
             if r >= OWN:
                 for half, v in enumerate(join(image[0], image[1])):
                     partial[level, half, r - OWN : r - OWN + 8, :] = v
+        if place == PLACES - 1:
+
+            @pl.when(turn == 0)
+            def _():
+                send_halo()
+
         beside_copy(level).start()
 
         @pl.when(level > 0)
@@ -463,27 +481,25 @@
             pass_on(level - 1)
 
     def run_turn(turn, carry):
-        @pl.when(turn == 0)
-        def _():
-            take_speeds(0, 1)
-            each_rim(0, (0, 1), start)
-            for owner in range(1, 4):
-                take_speeds(owner, owner + 1)
-                each_rim(0, (2 * owner, 2 * owner + 1)[: 7 - 2 * owner], start)
-
         @pl.when(turn == 1)
         def _():
-            send_halo()
+            for place in range(PLACES):
+                find_factors(turn, place)
             take_halo()
 
         for place in range(PLACES):
             advance(turn, place)
-            if place == 3:
-
-                @pl.when(turn == 0)
-                def _():
-                    take_speeds(4, 8)
-                    each_rim(1, range(7), start)
+            for after, first, last, round, places in (
+                (0, 2, 3, 0, (4, 5)),
+                (1, 3, 4, 0, (6,)),
+                (3, 4, 8, 1, range(7)),
+            ):
+                if place == after:
+
+                    @pl.when(turn == 0)
+                    def _():
+                        take_speeds(first, last)
+                        each_rim(round, places, start)
 
         return carry
 
@@ -562,7 +578,7 @@
             vmem(LEVELS, 2, 2, TILE, 128, dtype=jnp.int32),
             vmem(2, TERMS, 128),
             vmem(2 * TERMS, 8, 128),
-            vmem(2, FOLD, 128, dtype=jnp.int32),
+            vmem(PLACES, 2 * TERMS, 2 * FOLD, 128),
             vmem(LEVELS, 2, TILE, 128),
             vmem(LEVELS, TILE, 128),
             vmem(LEVELS, TILE, 128),

time: 61.4 us -> 56.9 us (0.927)
  Pallas kernels: 59.9 us -> 55.4 us
    pallas_call x1, Pallas kernels: 59.9 us -> 55.4 us  [body(): pl.pallas_call(kernel, out_shape=jax.ShapeDtypeStruct((2, TILE, 128), jnp...]
where the time goes in v3:
time: 56.9 us; the launch traced here: 56.8 us
  Pallas kernels  55.4 us (97%)
  local copies, waits for them, and re-layouts  1.38 us (2%)
    pallas_call x1, Pallas kernels, body(): pl.pallas_call(kernel, out_shape=jax.ShapeDtypeStruct((2, TILE, 128), jnp...  55.4 us
    unnamed x1, local copies, waits for them, and re-layouts  1.38 us

profile of v3, /device:TPU:6, one launch (start us, length us, event | category | flops | bytes accessed | tf_op | source)
XLA Modules:
  0.0 56.8 jit_solution(9303254014908413672)
XLA Ops:
  0.0 55.4 %shard_map.37 = f32[2,32,128]{2,1,0:T(8,128)} custom-call(f32[4,4,4,32,128]{4,3,2,1,0:T(8,128)} %bitcast.1, s32[2,32,128]{2,1,0:T(8,128)} %speeds.1, f32[16,2,8,128]{3,2,1,0:T(8,128)} %table.1), custom_call_target="tpu_custom_call" | custom-call | tf_op jit(solution)/shard_map/pallas_call | solution.py:567
  55.4 1.4 %copy.5 = f32[2,32,128]{2,1,0:T(8,128)} copy(f32[2,32,128]{2,1,0:T(8,128)} %shard_map.37) | data formatting | bytes 65536
